TPU v7x, 512 devices: a whole 4x4x16 slice. The times are simulated.
512 devices in a mesh: img: 16 (over x, y_hi, core), txt: 32 (over y_lo, z).
Axes of the slice: x: 4, y: 4 (y_hi: 2, y_lo: 2; y = y_hi * 2 + y_lo), z: 16, core: 2. Of those that a mesh axis runs over, the one named last changes fastest.
Arguments:
- image_rows: bfloat16 [262144, 1152], P(('img', 'txt')), may hold values from -6 to 6
- text_rows: bfloat16 [262144, 1152], P(('img', 'txt')), may hold values from -6 to 6
- image_ids: int32 [262144], P(('img', 'txt')), may hold values from 0 to 511
- text_ids: int32 [262144], P(('img', 'txt')), may hold values from 0 to 511
- log_scale: float32 [1], replicated, may hold values from 4 to 4.8
- logit_bias: float32 [1], replicated, may hold values from -12 to -6
Outputs:
- row_loss: float32 [262144], P(('img', 'txt'))
- image_grad: bfloat16 [262144, 1152], P(('img', 'txt'))
- text_grad: bfloat16 [262144, 1152], P(('img', 'txt'))
All inputs are finite; a program needn't handle non-finite values.
Results may differ from a plain program's by a relative error of at most 0.0078.
Values may be sent and summed in bfloat16 or wider, within the bound.
A program may use at most 64 MiB of HBM per device.

v0:
```python
import jax
import jax.numpy as jnp
from jax import lax
from jax.sharding import PartitionSpec as P


def passed_along(block, axis, distance):
    devices = range(lax.axis_size(axis))
    route = [((i - distance) % len(devices), i) for i in devices]
    return lax.ppermute(block, axis, route)


def unit_rows(block_rows):
    widened = block_rows.astype(jnp.float32)
    inverse = lax.rsqrt(jnp.sum(widened * widened, axis=1, keepdims=True) + 1e-06)
    return ((widened * inverse).astype(jnp.bfloat16), inverse)


def pair_terms(image_unit, text_unit, image_tags, text_tags, logit_scale, bias_value):
    logits = (
        logit_scale * jnp.dot(image_unit, text_unit.T, preferred_element_type=jnp.float32)
        + bias_value
    )
    pair_signs = jnp.where(image_tags[:, None] == text_tags[None, :], 1.0, -1.0).astype(jnp.float32)
    margins = pair_signs * logits
    losses = jnp.sum(jax.nn.softplus(-margins), axis=1)
    slopes = (-logit_scale * pair_signs * jax.nn.sigmoid(-margins)).astype(jnp.bfloat16)
    return (losses, slopes)


def across_rows(slopes, image_unit):
    return lax.dot_general(
        slopes, image_unit, (((0,), (0,)), ((), ())), preferred_element_type=jnp.float32
    )


def back_norm(block_rows, inverse, unit_grad):
    widened = block_rows.astype(jnp.float32)
    inner_sum = jnp.sum(widened * unit_grad, axis=1, keepdims=True)
    return (inverse * unit_grad - inverse * inverse * inverse * widened * inner_sum).astype(
        jnp.bfloat16
    )


def body(image_rows, text_rows, image_ids, text_ids, log_scale, logit_bias):
    logit_scale = jnp.exp(log_scale[0])
    bias_value = logit_bias[0]
    image_unit, image_inverse = unit_rows(image_rows)
    text_unit, text_inverse = unit_rows(text_rows)
    losses, slopes = pair_terms(image_unit, text_unit, image_ids, text_ids, logit_scale, bias_value)
    row_loss = losses
    image_acc = jnp.dot(slopes, text_unit, preferred_element_type=jnp.float32)
    text_acc = across_rows(slopes, image_unit)
    halfway = passed_along((text_unit, text_ids), "img", 1)
    visit_text, visit_text_tags = passed_along((halfway[0], halfway[1]), "txt", -1)
    losses, slopes = pair_terms(
        image_unit, visit_text, image_ids, visit_text_tags, logit_scale, bias_value
    )
    row_loss = row_loss + losses
    image_acc = image_acc + jnp.dot(slopes, visit_text, preferred_element_type=jnp.float32)
    text_part = across_rows(slopes, image_unit)
    returning = passed_along(text_part, "txt", 1)
    text_acc = text_acc + passed_along(returning, "img", -1)
    image_grad = back_norm(image_rows, image_inverse, image_acc)
    text_grad = back_norm(text_rows, text_inverse, text_acc)
    return (row_loss, image_grad, text_grad)


def solution(mesh):
    in_specs = (
        P(("img", "txt"), None),
        P(("img", "txt"), None),
        P(("img", "txt")),
        P(("img", "txt")),
        P(),
        P(),
    )
    out_specs = (P(("img", "txt")), P(("img", "txt"), None), P(("img", "txt"), None))
    return jax.shard_map(body, mesh=mesh, in_specs=in_specs, out_specs=out_specs, check_vma=False)
```

profile of v0, /device:TPU:1, one launch (start us, length us, event | category | flops | bytes accessed | tf_op | source)
XLA Modules:
  0.0 154.1 jit_solution(115248010584382512)
XLA Ops:
  0.6 0.0 copy-start.2
  0.6 0.0 copy-start.1
  0.7 1.7 %fusion.6 = f32[512]{0:T(512)S(1)} fusion(bf16[512,1152]{1,0:T(8,128)(2,1)} %param.7), kind=kLoop, calls=%fused_computation.17 | loop fusion | flops 1768960 | bytes 1181696 | tf_op jit(solution)/shard_map/reduce_sum | solution.py:15
  2.3 1.5 fusion.7
  3.9 6.2 %collective-permute-start.2 = (bf16[512,1152]{1,0:T(8,128)(2,1)S(1)}, bf16[512,1152]{1,0:T(8,128)(2,1)}, u32[]{:S(2)}, u32[]{:S(2)}) collective-permute-start(bf16[512,1152]{1,0:T(8,128)(2,1)S(1)} %fusion.7), channel_id=1, source_target_pairs={{480,0},{0,32},{32,64},{64,96},{96,128},{128,160},{160,192},{192,2... | collective-permute-start | bytes 3538952 | tf_op jit(solution)/shard_map/ppermute | solution.py:10
  10.1 13.1 %collective-permute-done.2 = bf16[512,1152]{1,0:T(8,128)(2,1)} collective-permute-done((bf16[512,1152]{1,0:T(8,128)(2,1)S(1)}, bf16[512,1152]{1,0:T(8,128)(2,1)}, u32[]{:S(2)}, u32[]{:S(2)}) %collective-permute-start.2) | collective-permute-done | bytes 1179680 | tf_op jit(solution)/shard_map/ppermute | solution.py:10
  23.2 11.2 %collective-permute-start.3 = (bf16[512,1152]{1,0:T(8,128)(2,1)}, bf16[512,1152]{1,0:T(8,128)(2,1)S(1)}, u32[]{:S(2)}, u32[]{:S(2)}) collective-permute-start(bf16[512,1152]{1,0:T(8,128)(2,1)} %collective-permute-done.2), channel_id=1, source_target_pairs={{1,0},{2,1},{3,2},{4,3},{5,4},{6,5},{7,6},{8,7},{9,8},{10,9},{11,1... | collective-permute-start | bytes 3538952 | tf_op jit(solution)/shard_map/ppermute | solution.py:10
  34.5 0.0 copy-done.2
  34.5 6.9 %collective-permute-start = (s32[512]{0:T(512)S(1)}, s32[512]{0:T(512)}, u32[]{:S(2)}, u32[]{:S(2)}) collective-permute-start(s32[512]{0:T(512)S(1)} %copy-done.2), channel_id=1, source_target_pairs={{480,0},{0,32},{32,64},{64,96},{96,128},{128,160},{160,192},{192,2... | collective-permute-start | bytes 6152 | tf_op jit(solution)/shard_map/ppermute | solution.py:10
  41.4 0.0 copy-done.1
  41.4 0.3 fusion
  41.7 0.4 collective-permute-done
  42.1 2.3 %collective-permute-start.1 = (s32[512]{0:T(512)}, s32[512]{0:T(512)}, u32[]{:S(2)}, u32[]{:S(2)}) collective-permute-start(s32[512]{0:T(512)} %collective-permute-done), channel_id=1, source_target_pairs={{1,0},{2,1},{3,2},{4,3},{5,4},{6,5},{7,6},{8,7},{9,8},{10,9},{11,1... | collective-permute-start | bytes 6152 | tf_op jit(solution)/shard_map/ppermute | solution.py:10
  45.7 10.0 %collective-permute-done.1 = s32[512]{0:T(512)} collective-permute-done((s32[512]{0:T(512)}, s32[512]{0:T(512)}, u32[]{:S(2)}, u32[]{:S(2)}) %collective-permute-start.1) | collective-permute-done | bytes 2080 | tf_op jit(solution)/shard_map/ppermute | solution.py:10
  55.7 0.0 collective-permute-done.3
  55.7 0.0 copy-start.4
  55.7 2.4 %fusion.19 = (f32[512]{0:T(512)S(1)}, f32[512,512]{0,1:T(8,128)S(1)}) fusion(f32[]{:T(128)} %bitcast.7, bf16[512,1152]{1,0:T(8,128)(2,1)S(1)} %collective-permute-done.3, bf16[512,1152]{1,0:T(8,128)(2,1)S(1)} %copy-done.1, f32[512]{0:T(512)S(1)} %get-tuple-element.6, f32[]{:T(128)} %bitcast, s32[512]{0:T(512)} %collective-permute-done.1, s32[512]{0:T(512)} %param.8), kind=kOutput, calls=%fused_computation.36 | convolution fusion | flops 609156608 | bytes 3416072 | tf_op jit(solution)/shard_map/dot_general | solution.py:21
  58.1 0.0 copy-done.4
  58.1 0.0 copy-start.3
  58.1 1.8 %fusion.20 = f32[512,1152]{1,0:T(8,128)S(1)} fusion(bf16[512,1152]{1,0:T(8,128)(2,1)S(1)} %copy-done.1, f32[512]{0:T(512)S(1)} %get-tuple-element.6, f32[512,512]{0,1:T(8,128)S(1)} %get-tuple-element.10, f32[]{:T(128)S(6)} %neg.25, s32[512]{0:T(512)S(1)} %copy-done.4, s32[512]{0:T(512)} %collective-permute-done.1), kind=kOutput, calls=%fused_computation.41 | convolution fusion | flops 607584256 | bytes 4593668 | tf_op jit(solution)/shard_map/dot_general | solution.py:32
  59.9 1.9 %collective-permute-start.4 = (f32[512,1152]{1,0:T(8,128)S(1)}, f32[512,1152]{1,0:T(8,128)S(1)}, u32[]{:S(2)}, u32[]{:S(2)}) collective-permute-start(f32[512,1152]{1,0:T(8,128)S(1)} %fusion.20), channel_id=1, source_target_pairs={{31,0},{0,1},{1,2},{2,3},{3,4},{4,5},{5,6},{6,7},{7,8},{8,9},{9,10... | collective-permute-start | bytes 7077896 | tf_op jit(solution)/shard_map/ppermute | solution.py:10
  61.9 50.4 %collective-permute-done.4 = f32[512,1152]{1,0:T(8,128)S(1)} collective-permute-done((f32[512,1152]{1,0:T(8,128)S(1)}, f32[512,1152]{1,0:T(8,128)S(1)}, u32[]{:S(2)}, u32[]{:S(2)}) %collective-permute-start.4) | collective-permute-done | bytes 2359328 | tf_op jit(solution)/shard_map/ppermute | solution.py:10
  112.3 7.9 %collective-permute-start.5 = (f32[512,1152]{1,0:T(8,128)S(1)}, f32[512,1152]{1,0:T(8,128)S(1)}, u32[]{:S(2)}, u32[]{:S(2)}) collective-permute-start(f32[512,1152]{1,0:T(8,128)S(1)} %collective-permute-done.4), channel_id=1, source_target_pairs={{32,0},{64,32},{96,64},{128,96},{160,128},{192,160},{224,192},{256... | collective-permute-start | bytes 7077896 | tf_op jit(solution)/shard_map/ppermute | solution.py:10
  120.2 0.0 copy-done.3
  120.2 1.6 %fusion.18 = (f32[512]{0:T(512)S(1)}, f32[512,512]{0,1:T(8,128)S(1)}) fusion(f32[]{:T(128)} %bitcast.6, bf16[512,1152]{1,0:T(8,128)(2,1)S(1)} %fusion.7, bf16[512,1152]{1,0:T(8,128)(2,1)S(1)} %copy-done.1, f32[512]{0:T(512)S(1)} %get-tuple-element.6, f32[]{:T(128)} %bitcast, s32[512]{0:T(512)S(1)} %copy-done.3, s32[512]{0:T(512)S(1)} %copy-done.4), kind=kOutput, calls=%fused_computation.35 | convolution fusion | flops 609156608 | bytes 3416072 | tf_op jit(solution)/shard_map/dot_general | solution.py:21
  121.8 1.0 fusion.29
  122.8 0.6 add.61
  123.4 2.0 %fusion.5 = (f32[512]{0:T(512)S(1)}, f32[512,1152]{1,0:T(8,128)S(1)}) fusion(bf16[512,1152]{1,0:T(8,128)(2,1)S(1)} %copy-done.1, f32[512,1152]{1,0:T(8,128)S(1)} %fusion.29, bf16[512,1152]{1,0:T(8,128)(2,1)S(1)} %collective-permute-done.3, f32[512,512]{0,1:T(8,128)S(1)} %get-tuple-element.10, f32[]{:T(128)S(6)} %neg.25, s32[512]{0:T(512)S(1)} %copy-done.4, ...), kind=kOutput, calls=%fused_computation.16 | convolution fusion | flops 608173568 | bytes 8132612 | tf_op jit(solution)/shard_map/dot_general | solution.py:60
  125.4 0.0 copy-start
  125.4 1.5 %fusion.4 = bf16[512,1152]{1,0:T(8,128)(2,1)} fusion(bf16[512,1152]{1,0:T(8,128)(2,1)S(1)} %copy-done.1, f32[512,1152]{1,0:T(8,128)S(1)} %get-tuple-element.12, f32[512]{0:T(512)S(1)} %get-tuple-element.11, f32[512]{0:T(512)S(1)} %get-tuple-element.5, f32[512]{0:T(512)S(1)} %get-tuple-element.6), kind=kLoop, calls=%fused_computation.15 | loop fusion | flops 3538944 | bytes 4724736 | tf_op jit(solution)/shard_map/convert_element_type | solution.py:40
  126.9 24.1 %collective-permute-done.5 = f32[512,1152]{1,0:T(8,128)S(1)} collective-permute-done((f32[512,1152]{1,0:T(8,128)S(1)}, f32[512,1152]{1,0:T(8,128)S(1)}, u32[]{:S(2)}, u32[]{:S(2)}) %collective-permute-start.5) | collective-permute-done | bytes 2359328 | tf_op jit(solution)/shard_map/ppermute | solution.py:10
  151.1 0.0 copy-done
  151.1 1.4 fusion.11
  152.5 1.6 %fusion.10 = bf16[512,1152]{1,0:T(8,128)(2,1)} fusion(bf16[512,1152]{1,0:T(8,128)(2,1)S(1)} %copy-done, f32[512]{0:T(512)S(1)} %get-tuple-element.13, f32[512]{0:T(512)S(1)} %get-tuple-element.3, f32[512]{0:T(512)S(1)} %get-tuple-element.4, f32[512,1152]{1,0:T(8,128)S(1)} %get-tuple-element.14, f32[512,1152]{1,0:T(8,128)S(1)} %collective-permute-done.5), kind=kLoop, calls=%fused_computation.21 | loop fusion | flops 4128768 | bytes 7084032 | tf_op jit(solution)/shard_map/convert_element_type | solution.py:40
  (2 shorter events, 0.0 us)
Async XLA Ops:
  0.6 33.8 %copy-start.2 = (s32[512]{0:T(512)S(1)}, s32[512]{0:T(512)}, u32[]{:S(2)}) copy-start(s32[512]{0:T(512)} %param.9) | copy-start | bytes 6148
  0.6 40.7 %copy-start.1 = (bf16[512,1152]{1,0:T(8,128)(2,1)S(1)}, bf16[512,1152]{1,0:T(8,128)(2,1)}, u32[]{:S(2)}) copy-start(bf16[512,1152]{1,0:T(8,128)(2,1)} %param.6) | copy-start | bytes 3538948
  3.9 19.3 %collective-permute-start.2 = (bf16[512,1152]{1,0:T(8,128)(2,1)S(1)}, bf16[512,1152]{1,0:T(8,128)(2,1)}, u32[]{:S(2)}, u32[]{:S(2)}) collective-permute-start(bf16[512,1152]{1,0:T(8,128)(2,1)S(1)} %fusion.7), channel_id=1, source_target_pairs={{480,0},{0,32},{32,64},{64,96},{96,128},{128,160},{160,192},{192,2... | collective-permute-start | bytes 3538952 | tf_op jit(solution)/shard_map/ppermute | solution.py:10
  23.2 32.5 %collective-permute-start.3 = (bf16[512,1152]{1,0:T(8,128)(2,1)}, bf16[512,1152]{1,0:T(8,128)(2,1)S(1)}, u32[]{:S(2)}, u32[]{:S(2)}) collective-permute-start(bf16[512,1152]{1,0:T(8,128)(2,1)} %collective-permute-done.2), channel_id=1, source_target_pairs={{1,0},{2,1},{3,2},{4,3},{5,4},{6,5},{7,6},{8,7},{9,8},{10,9},{11,1... | collective-permute-start | bytes 3538952 | tf_op jit(solution)/shard_map/ppermute | solution.py:10
  34.5 7.6 %collective-permute-start = (s32[512]{0:T(512)S(1)}, s32[512]{0:T(512)}, u32[]{:S(2)}, u32[]{:S(2)}) collective-permute-start(s32[512]{0:T(512)S(1)} %copy-done.2), channel_id=1, source_target_pairs={{480,0},{0,32},{32,64},{64,96},{96,128},{128,160},{160,192},{192,2... | collective-permute-start | bytes 6152 | tf_op jit(solution)/shard_map/ppermute | solution.py:10
  42.1 13.6 %collective-permute-start.1 = (s32[512]{0:T(512)}, s32[512]{0:T(512)}, u32[]{:S(2)}, u32[]{:S(2)}) collective-permute-start(s32[512]{0:T(512)} %collective-permute-done), channel_id=1, source_target_pairs={{1,0},{2,1},{3,2},{4,3},{5,4},{6,5},{7,6},{8,7},{9,8},{10,9},{11,1... | collective-permute-start | bytes 6152 | tf_op jit(solution)/shard_map/ppermute | solution.py:10
  55.7 2.4 %copy-start.4 = (s32[512]{0:T(512)S(1)}, s32[512]{0:T(512)}, u32[]{:S(2)}) copy-start(s32[512]{0:T(512)} %param.8) | copy-start | bytes 6148
  58.1 62.1 %copy-start.3 = (s32[512]{0:T(512)S(1)}, s32[512]{0:T(512)}, u32[]{:S(2)}) copy-start(s32[512]{0:T(512)} %param.9) | copy-start | bytes 6148
  59.9 52.4 %collective-permute-start.4 = (f32[512,1152]{1,0:T(8,128)S(1)}, f32[512,1152]{1,0:T(8,128)S(1)}, u32[]{:S(2)}, u32[]{:S(2)}) collective-permute-start(f32[512,1152]{1,0:T(8,128)S(1)} %fusion.20), channel_id=1, source_target_pairs={{31,0},{0,1},{1,2},{2,3},{3,4},{4,5},{5,6},{6,7},{7,8},{8,9},{9,10... | collective-permute-start | bytes 7077896 | tf_op jit(solution)/shard_map/ppermute | solution.py:10
  112.3 38.8 %collective-permute-start.5 = (f32[512,1152]{1,0:T(8,128)S(1)}, f32[512,1152]{1,0:T(8,128)S(1)}, u32[]{:S(2)}, u32[]{:S(2)}) collective-permute-start(f32[512,1152]{1,0:T(8,128)S(1)} %collective-permute-done.4), channel_id=1, source_target_pairs={{32,0},{64,32},{96,64},{128,96},{160,128},{192,160},{224,192},{256... | collective-permute-start | bytes 7077896 | tf_op jit(solution)/shard_map/ppermute | solution.py:10
  125.4 25.7 %copy-start = (bf16[512,1152]{1,0:T(8,128)(2,1)S(1)}, bf16[512,1152]{1,0:T(8,128)(2,1)}, u32[]{:S(2)}) copy-start(bf16[512,1152]{1,0:T(8,128)(2,1)} %param.7) | copy-start | bytes 3538948
where the time goes:
time: 154 us
  waiting for transfers between devices  98.1 us (64%)
  starting transfers between devices  36.4 us (24%)
  matrix products  10.2 us (7%)
  other arithmetic  7.28 us (5%)
  between operations  2.11 us (1%)
    ppermute x6, waiting for transfers between devices, passed_along(): return lax.ppermute(block, axis, route)  98.1 us
    ppermute x6, starting transfers between devices, passed_along(): return lax.ppermute(block, axis, route)  36.4 us
    dot_general x2, matrix products, pair_terms(): jnp.dot(image_unit, text_unit.T, preferred_element_type=jnp.float32)  4.01 us
    dot_general x2, matrix products, across_rows(): lax.dot_general(slopes, image_unit, (((0,), (0,)), ((), ())), preferred_e...  3.21 us
    convert_element_type x2, other arithmetic, back_norm(): (inverse * unit_grad - inverse * inverse * inverse * widened * inner_sum)...  3.17 us
  transfers between devices with their start and end apart: 6, of which 5 were waited for; matrix products, arithmetic and copies ran while one was open for 5% of the time, Pallas kernels for 0%

commit v1 on v0

v1 whole, which is shorter than its diff:
```python
import functools

import jax
import jax.numpy as jnp
from jax import lax
from jax.experimental import pallas as pl
from jax.experimental.pallas import tpu as pltpu
from jax.sharding import PartitionSpec as P

MESH = pl.DeviceIdType.MESH
ROWS, D = 512, 1152
C = 128
CHUNKS = ROWS // C
NEAR, FAR = 0, 1


def inverse_norm(x):
    return lax.rsqrt(jnp.sum(x * x, axis=1, keepdims=True) + 1e-06)


def kernel(
    img, txt, img_ids, txt_ids, log_scale, logit_bias,
    loss_out, img_out, txt_out,
    own, unit, inv, got, acc, own_ids, got_ids, id_col, id_row, loss_acc,
    own_sem, own_id_sem, send_sem, recv_sem, id_send_sem, id_recv_sem,
):
    n_img, n_txt = lax.axis_size("img"), lax.axis_size("txt")
    p, q = lax.axis_index("img"), lax.axis_index("txt")
    core = lax.rem(p, 2)
    text_to = (lax.rem(p + 1, n_img), lax.rem(q + n_txt - 1, n_txt))
    image_to = (lax.rem(p + n_img - 1, n_img), lax.rem(q + 1, n_txt))

    barrier = pltpu.get_barrier_semaphore()
    for partner in (text_to, image_to):
        pl.semaphore_signal(barrier, inc=1, device_id=partner, device_id_type=MESH)

    def local_loads(sides):
        copies = []
        for side, (rows, ids) in enumerate(sides):
            copies.append(pltpu.make_async_copy(ids, own_ids.at[side], own_id_sem.at[side]))
            copies.append(pltpu.make_async_copy(rows, own.at[side], own_sem.at[side]))
        return copies

    def sends(sides, targets):
        copies = []
        for side, (rows, ids) in enumerate(sides):
            copies.append(
                pltpu.make_async_remote_copy(
                    src_ref=ids, dst_ref=got_ids.at[side],
                    send_sem=id_send_sem.at[side], recv_sem=id_recv_sem.at[side],
                    device_id=targets[side], device_id_type=MESH,
                )
            )
        for k in range(CHUNKS):
            for side, (rows, ids) in enumerate(sides):
                piece = pl.ds(k * C, C)
                copies.append(
                    pltpu.make_async_remote_copy(
                        src_ref=rows.at[piece], dst_ref=got.at[side, piece],
                        send_sem=send_sem.at[side, k], recv_sem=recv_sem.at[side, k],
                        device_id=targets[side], device_id_type=MESH,
                    )
                )
        return copies

    by_core = (
        (((txt, txt_ids), (img, img_ids)), (text_to, image_to)),
        (((img, img_ids), (txt, txt_ids)), (image_to, text_to)),
    )
    for c, (sides, targets) in enumerate(by_core):

        @pl.when(core == c)
        def _():
            for copy in local_loads(sides):
                copy.start()

    with jax.named_scope("barrier_wait"):
        pl.semaphore_wait(barrier, 2)

    for c, (sides, targets) in enumerate(by_core):

        @pl.when(core == c)
        def _():
            for copy in sends(sides, targets):
                copy.start()

    scale = jnp.exp(jnp.full((1, C), log_scale[0], jnp.float32))
    bias = logit_bias[0]

    for c, (sides, targets) in enumerate(by_core):

        @pl.when(core == c)
        def _():
            for copy in local_loads(sides):
                copy.wait()

    for side in (NEAR, FAR):
        for k in range(CHUNKS):
            piece = pl.ds(k * C, C)
            row = own_ids[side, piece].reshape(1, C)
            id_row[side, k] = jnp.broadcast_to(row, (8, C))
            id_col[side, piece, :] = jnp.broadcast_to(row, (C, C)).T

        @pl.loop(0, CHUNKS)
        def _(k):
            piece = pl.ds(k * C, C)
            x = own[side, piece, :].astype(jnp.float32)
            r = inverse_norm(x)
            inv[side, piece, :] = r
            unit[side, piece, :] = (x * r).astype(jnp.bfloat16)

    loss_acc[...] = jnp.zeros_like(loss_acc)
    acc[...] = jnp.zeros_like(acc)

    def slopes_of(side, other_unit, other_id_row, has_loss):
        logits = (
            lax.dot_general(
                unit[side], other_unit, (((1,), (1,)), ((), ())), preferred_element_type=jnp.float32
            )
            * scale
            + bias
        )
        same = id_col[side] == other_id_row
        margins = jnp.where(same, logits, -logits)
        e = jnp.exp(-jnp.abs(margins))
        recip = 1.0 / (1.0 + e)
        sigmoid = jnp.where(margins >= 0, e * recip, recip)

        @pl.when(has_loss)
        def _():
            loss_acc[...] += jnp.maximum(-margins, 0.0) + jnp.log1p(e)

        return (jnp.where(same, -scale, scale) * sigmoid).astype(jnp.bfloat16)

    def add_product(side, slopes, other_unit):
        acc[side] += jnp.dot(slopes, other_unit, preferred_element_type=jnp.float32)

    def has_loss(side):
        return core == (1 if side == NEAR else 0)

    for side in (NEAR, FAR):

        @pl.loop(0, CHUNKS)
        @jax.named_scope("own_pair_chunk")
        def _(k):
            other = unit[1 - side, pl.ds(k * C, C), :]
            slopes = slopes_of(side, other, id_row[1 - side, k][0:1], has_loss(side))
            add_product(side, slopes, other)

    for side in (NEAR, FAR):
        pltpu.make_async_remote_copy(
            src_ref=own_ids.at[side], dst_ref=got_ids.at[side],
            send_sem=id_send_sem.at[side], recv_sem=id_recv_sem.at[side],
            device_id=text_to, device_id_type=MESH,
        ).wait_recv()
        for k in range(CHUNKS):
            row = got_ids[side, pl.ds(k * C, C)].reshape(1, C)
            id_row[side, k] = jnp.broadcast_to(row, (8, C))

    def arrived(side, k):
        piece = pl.ds(k * C, C)
        pltpu.make_async_remote_copy(
            src_ref=own.at[side, piece], dst_ref=got.at[side, piece],
            send_sem=send_sem.at[side, k], recv_sem=recv_sem.at[side, k],
            device_id=text_to, device_id_type=MESH,
        ).wait_recv()
        x = got[side, piece, :].astype(jnp.float32)
        return (x * inverse_norm(x)).astype(jnp.bfloat16)

    @pl.loop(0, CHUNKS - 1)
    def _(k):
        for side, name in ((NEAR, "near"), (FAR, "far")):
            with jax.named_scope(f"{name}_chunk_wait"):
                other = arrived(side, k)
            with jax.named_scope(f"{name}_chunk"):
                slopes = slopes_of(side, other, id_row[side, k][0:1], has_loss(side))
                add_product(side, slopes, other)

    def finish(side, slopes, other, out):
        step = 128
        for b in range(ROWS // step):
            rows = pl.ds(b * step, step)
            g = acc[side, rows, :] + jnp.dot(
                slopes[b * step : (b + 1) * step], other, preferred_element_type=jnp.float32
            )
            x = own[side, rows, :].astype(jnp.float32)
            r = inv[side, rows, :]
            inner = jnp.sum(x * g, axis=1, keepdims=True)
            out[rows, :] = (r * g - (r * r * r * inner) * x).astype(jnp.bfloat16)

    for side, name in ((NEAR, "near"), (FAR, "far")):
        with jax.named_scope(f"last_{name}_chunk_wait"):
            other = arrived(side, CHUNKS - 1)
        with jax.named_scope(f"finish_{name}_side"):
            slopes = slopes_of(side, other, id_row[side, CHUNKS - 1][0:1], has_loss(side))
            for c, outs in enumerate(((txt_out, img_out), (img_out, txt_out))):
                pl.when(core == c)(functools.partial(finish, side, slopes, other, outs[side]))

    with jax.named_scope("loss_and_send_waits"):
        loss_out[...] = jnp.sum(loss_acc[...].T, axis=0, keepdims=True).reshape(ROWS)
        for c, (sides, targets) in enumerate(by_core):

            @pl.when(core == c)
            def _():
                for copy in sends(sides, targets):
                    copy.wait_send()


def body(image_rows, text_rows, image_ids, text_ids, log_scale, logit_bias):
    bf16, f32, i32 = jnp.bfloat16, jnp.float32, jnp.int32
    hbm = pl.BlockSpec(memory_space=pltpu.HBM)
    vmem = pl.BlockSpec(memory_space=pltpu.VMEM)
    operands = [
        pltpu.with_memory_space_constraint(x, pltpu.HBM)
        for x in (image_rows, text_rows, image_ids, text_ids)
    ]
    dma = pltpu.SemaphoreType.DMA
    return pl.pallas_call(
        kernel,
        out_shape=(
            pltpu.VMEM((ROWS,), f32),
            pltpu.VMEM((ROWS, D), bf16),
            pltpu.VMEM((ROWS, D), bf16),
        ),
        in_specs=[hbm] * 4 + [pl.BlockSpec(memory_space=pltpu.SMEM)] * 2,
        out_specs=(vmem,) * 3,
        scratch_shapes=[
            pltpu.VMEM((2, ROWS, D), bf16),
            pltpu.VMEM((2, ROWS, D), bf16),
            pltpu.VMEM((2, ROWS, 1), f32),
            pltpu.VMEM((2, ROWS, D), bf16),
            pltpu.VMEM((2, ROWS, D), f32),
            pltpu.VMEM((2, ROWS), i32),
            pltpu.VMEM((2, ROWS), i32),
            pltpu.VMEM((2, ROWS, C), i32),
            pltpu.VMEM((2, CHUNKS, 8, C), i32),
            pltpu.VMEM((ROWS, C), f32),
            dma((2,)), dma((2,)), dma((2, CHUNKS)), dma((2, CHUNKS)), dma((2,)), dma((2,)),
        ],
        compiler_params=pltpu.CompilerParams(
            collective_id=0, has_side_effects=True, vmem_limit_bytes=40 << 20
        ),
        name="exchange_and_grads",
    )(*operands, log_scale, logit_bias)


def solution(mesh):
    blocks = P(("img", "txt"))
    rows = P(("img", "txt"), None)
    return jax.shard_map(
        body,
        mesh=mesh,
        in_specs=(rows, rows, blocks, blocks, P(), P()),
        out_specs=(blocks, rows, rows),
        check_vma=False,
    )
```

time: 154 us -> 47.4 us (0.31)
  waiting for transfers between devices: 98.1 us -> 0 us
  Pallas kernels: 0 us -> 42.6 us
  starting transfers between devices: 36.4 us -> 0 us
  matrix products: 10.2 us -> 0 us
  other arithmetic: 7.28 us -> 0 us
  local copies, waits for them, and re-layouts: 0.02 us -> 2.61 us
    ppermute x6 -> x0, waiting for transfers between devices: 98.1 us -> none  [passed_along(): return lax.ppermute(block, axis, route)]
    pallas_call x0 -> x1, Pallas kernels: none -> 42.6 us  [body(): pl.pallas_call(kernel, out_shape=(pltpu.VMEM((ROWS,), f32), pltpu.VMEM((R...]
    ppermute x6 -> x0, starting transfers between devices: 36.4 us -> none  [passed_along(): return lax.ppermute(block, axis, route)]
    dot_general x6 -> x0, matrix products: 10.2 us -> none  [the longest x2 4.01 us: pair_terms(): jnp.dot(image_unit, text_unit.T, preferred_element_type=jnp.float32)]
    convert_element_type x3 -> x0, other arithmetic: 4.7 us -> none  [the longest x2 3.17 us: back_norm(): (inverse * unit_grad - inverse * inverse * inverse * widened * inner_sum)...]
    unnamed x10 -> x3, local copies, waits for them, and re-layouts: 0.02 us -> 2.61 us
    reduce_sum x2 -> x0, other arithmetic: 1.98 us -> none  [unit_rows(): jnp.sum(widened * widened, axis=1, keepdims=True) + 1e-06]
  transfers between devices with their start and end apart: 6 -> 0, of which waited for: 5 -> 0; matrix products, arithmetic and copies ran while one was open for 5% -> 0% of each run, Pallas kernels for 0% -> 0%
where the time goes in v1:
time: 47.4 us; the launch traced here: 47.1 us
  Pallas kernels  42.6 us (90%)
  local copies, waits for them, and re-layouts  2.61 us (6%)
  between operations  1.93 us (4%)
    pallas_call x1, Pallas kernels, body(): pl.pallas_call(kernel, out_shape=(pltpu.VMEM((ROWS,), f32), pltpu.VMEM((R...  42.6 us
    unnamed x3, local copies, waits for them, and re-layouts  2.61 us

profile of v1, /device:TPU:1, one launch (start us, length us, event | category | flops | bytes accessed | tf_op | source)
XLA Modules:
  0.0 47.1 jit_solution(14589628641953548887)
XLA Ops:
  1.9 42.6 %exchange_and_grads.1 = (f32[512]{0:T(512)S(1)}, bf16[512,1152]{1,0:T(8,128)(2,1)S(1)}, bf16[512,1152]{1,0:T(8,128)(2,1)S(1)}) custom-call(bf16[512,1152]{1,0:T(8,128)(2,1)} %img.1, bf16[512,1152]{1,0:T(8,128)(2,1)} %txt.1, s32[512]{0:T(512)} %img_ids.1, s32[512]{0:T(512)} %txt_ids.1, f32[1]{0:T(128)S(6)} %copy.15.log_scale, f32[1]{0:T(128)S(6)} %copy.16.logit_bias), custom_call_target="tpu_custom_call" | custom-call | tf_op jit(solution)/shard_map/exchange_and_grads/pallas_call | solution.py:218
  44.5 0.6 %copy.12 = f32[512]{0:T(512)} copy(f32[512]{0:T(512)S(1)} %get-tuple-element.3) | data formatting | bytes 4096
  45.1 1.0 %copy.13 = bf16[512,1152]{1,0:T(8,128)(2,1)} copy(bf16[512,1152]{1,0:T(8,128)(2,1)S(1)} %get-tuple-element.4) | data formatting | bytes 2359296
  46.1 1.0 %copy.14 = bf16[512,1152]{1,0:T(8,128)(2,1)} copy(bf16[512,1152]{1,0:T(8,128)(2,1)S(1)} %get-tuple-element.5) | data formatting | bytes 2359296

commit v2 on v0

v2 whole, which is shorter than its diff:
```python
import jax
import jax.numpy as jnp
from jax import lax
from jax.experimental import pallas as pl
from jax.experimental.pallas import tpu as pltpu
from jax.sharding import PartitionSpec as P

MESH = pl.DeviceIdType.MESH
ROWS, D = 512, 1152
C = 128
FULL = ROWS // C - 1
HALF = C // 2
BLOCK = 128
TEXT, IMAGE = 0, 1


def inverse_norm(x):
    return lax.rsqrt(jnp.sum(x * x, axis=1, keepdims=True) + 1e-06)


def unit_rows(rows):
    x = rows.astype(jnp.float32)
    return (x * inverse_norm(x)).astype(jnp.bfloat16)


def slopes_of(own_unit, other_unit, same, scale, bias):
    dots = lax.dot_general(
        own_unit, other_unit, (((1,), (1,)), ((), ())), preferred_element_type=jnp.float32
    )
    logits = dots * scale + bias
    margins = jnp.where(same, logits, -logits)
    e = jnp.exp(-jnp.abs(margins))
    recip = 1.0 / (1.0 + e)
    sigmoid = jnp.where(margins >= 0, e * recip, recip)
    slopes = (jnp.where(same, -scale, scale) * sigmoid).astype(jnp.bfloat16)
    return slopes, dots, lambda: jnp.maximum(-margins, 0.0) + jnp.log1p(e)


def back_norm(rows, r, g):
    x = rows.astype(jnp.float32)
    inner = jnp.sum(x * g, axis=1, keepdims=True)
    return r * g - (r * r * r * inner) * x


def exchange_kernel(
    img, txt, img_ids, txt_ids, log_scale, logit_bias,
    loss, image_grad, text_own, text_unit, text_inv, text_base, last_unit, text_id_col, last_id_row, constants,
    image_own, image_unit, image_inv, image_acc, got, own_ids, got_ids, image_id_col, id_row, loss_acc,
    own_sem, own_id_sem, send_sem, recv_sem, id_send_sem, id_recv_sem, ack_sem,
):
    n_img, n_txt = lax.axis_size("img"), lax.axis_size("txt")
    p, q = lax.axis_index("img"), lax.axis_index("txt")
    text_to = (lax.rem(p + 1, n_img), lax.rem(q + n_txt - 1, n_txt))
    image_to = (lax.rem(p + n_img - 1, n_img), lax.rem(q + 1, n_txt))

    n_z = n_txt // 2
    z, core, y_hi = lax.rem(q, n_z), lax.rem(p, 2), lax.rem(p // 2, 2)
    near_to = (jnp.where(core == 0, text_to[0], image_to[0]), jnp.where(core == 0, text_to[1], image_to[1]))
    far_to = (jnp.where(core == 0, image_to[0], text_to[0]), jnp.where(core == 0, image_to[1], text_to[1]))
    first, last = jnp.int32(z == 0), jnp.int32(z == n_z - 1)
    both = jnp.where(core == 0, y_hi, 1 - y_hi)
    from_last = jnp.maximum(first, last)
    to_last = jnp.maximum(jnp.int32(z == n_z - 2), last)
    near_signals = jnp.where(core == 0, from_last, 1 - to_last)
    near_direct = 1 - near_signals
    near_acks = near_direct
    far_signals = jnp.where(core == 0, 1 - to_last, jnp.maximum(from_last, both))
    far_direct = jnp.where(core == 0, jnp.maximum(to_last, both), 1 - from_last)
    far_acks = jnp.where(core == 0, to_last, (1 - from_last) * (1 - both))
    image_direct = jnp.where(core == 0, far_direct, near_direct)
    text_direct = jnp.where(core == 0, near_direct, far_direct)

    barrier = pltpu.get_barrier_semaphore()
    for signals, partner in ((near_signals, near_to), (far_signals, far_to)):

        @pl.when(signals == 1)
        def _():
            pl.semaphore_signal(barrier, inc=1, device_id=partner, device_id_type=MESH)

    sources, source_ids, targets = (txt, img), (txt_ids, img_ids), (text_to, image_to)
    own, unit, inv, acc = (
        (image_own, text_own), (image_unit, text_unit), (image_inv, text_inv), (image_acc, text_base),
    )
    id_col = (image_id_col, text_id_col)
    pieces = (
        [(k * C, C) for k in range(FULL + 1)],
        [(k * C, C) for k in range(FULL)] + [(FULL * C, HALF), (FULL * C + HALF, HALF)],
    )

    def id_copy(side):
        return pltpu.make_async_remote_copy(
            src_ref=source_ids[side], dst_ref=got_ids.at[side],
            send_sem=id_send_sem.at[side], recv_sem=id_recv_sem.at[side],
            device_id=targets[side], device_id_type=MESH,
        )

    def piece_copy(side, k, start, size):
        rows = pl.ds(start, size)
        return pltpu.make_async_remote_copy(
            src_ref=sources[side].at[rows], dst_ref=got.at[side, rows],
            send_sem=send_sem.at[side, k], recv_sem=recv_sem.at[side, k],
            device_id=targets[side], device_id_type=MESH,
        )

    def sends(side):
        return [id_copy(side)] + [piece_copy(side, k, *piece) for k, piece in enumerate(pieces[side])]

    loads = []
    for side, ref, ids in ((TEXT, img, img_ids), (IMAGE, txt, txt_ids)):
        loads.append(pltpu.make_async_copy(ids, own_ids.at[side], own_id_sem.at[side]))
        loads.append(pltpu.make_async_copy(ref, own[side], own_sem.at[side]))
    for copy in loads:
        copy.start()

    def start_sends(side):
        for copy in sends(side):
            copy.start()

    n_direct = near_direct + far_direct

    @pl.when(n_direct > 0)
    def _():
        pl.semaphore_wait(barrier, n_direct)

    for i, (acks, partner) in enumerate(((near_acks, near_to), (far_acks, far_to))):

        @pl.when(acks == 1)
        def _():
            pl.semaphore_signal(ack_sem.at[i], inc=1, device_id=partner, device_id_type=MESH)

    image_ack = jnp.where(core == 0, 1, 0)
    pl.when(image_direct == 1)(lambda: start_sends(IMAGE))
    pl.when(text_direct == 1)(lambda: start_sends(TEXT))
    for side, direct, ack in ((IMAGE, image_direct, image_ack), (TEXT, text_direct, 1 - image_ack)):

        @pl.when(direct == 0)
        def _():
            pl.semaphore_wait(ack_sem.at[ack], 1)
            start_sends(side)

    scale = jnp.exp(jnp.full((1, C), log_scale[0], jnp.float32))
    bias = jnp.full((1, C), logit_bias[0], jnp.float32)
    constants[0:1, :] = scale
    constants[1:2, :] = bias

    for copy in loads:
        copy.wait()

    for side in (TEXT, IMAGE):
        for k in range(FULL + 1):
            piece = pl.ds(k * C, C)
            row = own_ids[side, piece].reshape(1, C)
            id_row[1 - side, k] = jnp.broadcast_to(row, (8, C))
            id_col[side][piece, :] = jnp.broadcast_to(row, (C, C)).T

        @pl.loop(0, FULL + 1)
        def _(k):
            piece = pl.ds(k * C, C)
            x = own[side][piece, :].astype(jnp.float32)
            r = inverse_norm(x)
            inv[side][piece, :] = jnp.broadcast_to(r, (C, C))
            unit[side][piece, :] = (x * r).astype(jnp.bfloat16)

    loss_acc[...] = jnp.zeros_like(loss_acc)
    for side in (TEXT, IMAGE):
        acc[side][...] = jnp.zeros_like(acc[side])

    def slopes_on(side, other_unit, other_ids):
        width = other_unit.shape[0]
        same = id_col[side][:, :width] == other_ids
        slopes, _, loss_terms = slopes_of(unit[side][...], other_unit, same, scale[:, :width], bias[:, :width])
        if side == TEXT:
            loss_acc[...] += loss_terms()
        return slopes

    def add_chunk(side, other_unit, other_ids):
        slopes = slopes_on(side, other_unit, other_ids)
        acc[side][...] += jnp.dot(slopes, other_unit, preferred_element_type=jnp.float32)

    for side in (TEXT, IMAGE):

        @pl.loop(0, FULL + 1)
        def _(k):
            add_chunk(side, unit[1 - side][pl.ds(k * C, C), :], id_row[side, k][0:1])

    for side in (TEXT, IMAGE):
        id_copy(side).wait_recv()
        for k in range(FULL + 1):
            row = got_ids[side, pl.ds(k * C, C)].reshape(1, C)
            id_row[side, k] = jnp.broadcast_to(row, (8, C))

    def arrived(side, k, start, size):
        piece_copy(side, k, start, size).wait_recv()
        return unit_rows(got[side, pl.ds(start, size), :])

    @pl.loop(0, FULL)
    def _(k):
        for side in (TEXT, IMAGE):
            other = arrived(side, k, k * C, C)
            add_chunk(side, other, id_row[side, k][0:1])

    def finish_text():
        other = arrived(TEXT, FULL, FULL * C, C)
        slopes = slopes_on(TEXT, other, id_row[TEXT, FULL][0:1])
        for b in range(ROWS // BLOCK):
            rows = pl.ds(b * BLOCK, BLOCK)
            g = image_acc[rows, :] + jnp.dot(
                slopes[b * BLOCK : (b + 1) * BLOCK], other, preferred_element_type=jnp.float32
            )
            grad = back_norm(image_own[rows, :], image_inv[rows, 0:1], g)
            image_grad[rows, :] = grad.astype(jnp.bfloat16)
        loss[...] = jnp.sum(loss_acc[...].T, axis=0, keepdims=True).reshape(ROWS)

    pl.when(first == 1)(finish_text)

    other = arrived(IMAGE, FULL, FULL * C, HALF)
    last_ids = id_row[IMAGE, FULL]
    add_chunk(IMAGE, other, last_ids[0:1, :HALF])
    last_id_row[...] = jnp.broadcast_to(last_ids[0:1, HALF:], (8, HALF))
    for b in range(ROWS // BLOCK):
        rows = pl.ds(b * BLOCK, BLOCK)
        text_base[rows, :] = back_norm(text_own[rows, :], text_inv[rows, 0:1], text_base[rows, :])

    pl.when(first == 0)(finish_text)

    for side in (TEXT, IMAGE):
        for copy in sends(side):
            copy.wait_send()
    last_unit[...] = arrived(IMAGE, FULL + 1, FULL * C + HALF, HALF)


def finish_kernel(
    loss, image_grad, own, unit, inv, base, last_unit, id_col, last_id_row, constants,
    loss_out, image_out, text_out,
    stage, sem,
):
    copies = [
        pltpu.make_async_copy(loss, loss_out, sem.at[0]),
        pltpu.make_async_copy(image_grad, image_out, sem.at[1]),
    ]
    for copy in copies:
        copy.start()
    other = last_unit[...]
    scale, bias = constants[0:1, :HALF], constants[1:2, :HALF]

    def slopes_and_inner(b):
        rows = pl.ds(b * BLOCK, BLOCK)
        same = id_col[rows, :HALF] == last_id_row[0:1]
        slopes, dots, _ = slopes_of(unit[rows, :], other, same, scale, bias)
        return slopes, jnp.sum(slopes.astype(jnp.float32) * dots, axis=1, keepdims=True)

    blocks = ROWS // BLOCK
    ahead = slopes_and_inner(0)
    for b in range(blocks):
        slopes, inner = ahead
        if b + 1 < blocks:
            ahead = slopes_and_inner(b + 1)
        rows = pl.ds(b * BLOCK, BLOCK)
        r = inv[rows, 0:1]
        h = jnp.dot(slopes, other, preferred_element_type=jnp.float32)
        grad = base[rows, :] + r * h - (r * r * inner) * own[rows, :].astype(jnp.float32)
        stage[rows, :] = grad.astype(jnp.bfloat16)
        copy = pltpu.make_async_copy(stage.at[rows], text_out.at[rows], sem.at[2 + b])
        copy.start()
        copies.append(copy)
    for copy in copies:
        copy.wait()


def body(image_rows, text_rows, image_ids, text_ids, log_scale, logit_bias):
    bf16, f32, i32 = jnp.bfloat16, jnp.float32, jnp.int32
    hbm = pl.BlockSpec(memory_space=pltpu.HBM)
    vmem = pl.BlockSpec(memory_space=pltpu.VMEM)
    smem = pl.BlockSpec(memory_space=pltpu.SMEM)
    dma = pltpu.SemaphoreType.DMA
    operands = [
        pltpu.with_memory_space_constraint(x, pltpu.HBM)
        for x in (image_rows, text_rows, image_ids, text_ids)
    ]
    handed_on = (
        pltpu.VMEM((ROWS,), f32),
        pltpu.VMEM((ROWS, D), bf16),
        pltpu.VMEM((ROWS, D), bf16),
        pltpu.VMEM((ROWS, D), bf16),
        pltpu.VMEM((ROWS, C), f32),
        pltpu.VMEM((ROWS, D), f32),
        pltpu.VMEM((HALF, D), bf16),
        pltpu.VMEM((ROWS, C), i32),
        pltpu.VMEM((8, HALF), i32),
        pltpu.VMEM((8, C), f32),
    )
    held = pl.pallas_call(
        exchange_kernel,
        out_shape=handed_on,
        in_specs=[hbm] * 4 + [smem] * 2,
        out_specs=(vmem,) * len(handed_on),
        scratch_shapes=[
            pltpu.VMEM((ROWS, D), bf16),
            pltpu.VMEM((ROWS, D), bf16),
            pltpu.VMEM((ROWS, C), f32),
            pltpu.VMEM((ROWS, D), f32),
            pltpu.VMEM((2, ROWS, D), bf16),
            pltpu.VMEM((2, ROWS), i32),
            pltpu.VMEM((2, ROWS), i32),
            pltpu.VMEM((ROWS, C), i32),
            pltpu.VMEM((2, FULL + 1, 8, C), i32),
            pltpu.VMEM((ROWS, C), f32),
            dma((2,)), dma((2,)), dma((2, FULL + 2)), dma((2, FULL + 2)), dma((2,)), dma((2,)),
            pltpu.SemaphoreType.REGULAR((2,)),
        ],
        compiler_params=pltpu.CompilerParams(
            collective_id=0, has_side_effects=True, vmem_limit_bytes=28 << 20
        ),
        name="exchange_and_grads",
    )(*operands, log_scale, logit_bias)
    held = [pltpu.with_memory_space_constraint(x, pltpu.VMEM) for x in held]
    return pl.pallas_call(
        finish_kernel,
        out_shape=(pltpu.HBM((ROWS,), f32), pltpu.HBM((ROWS, D), bf16), pltpu.HBM((ROWS, D), bf16)),
        in_specs=[vmem] * len(handed_on),
        out_specs=(hbm,) * 3,
        scratch_shapes=[pltpu.VMEM((ROWS, D), bf16), dma((2 + ROWS // BLOCK,))],
        compiler_params=pltpu.CompilerParams(vmem_limit_bytes=12 << 20),
        name="finish_text_side",
    )(*held)


def solution(mesh):
    blocks = P(("img", "txt"))
    rows = P(("img", "txt"), None)
    return jax.shard_map(
        body,
        mesh=mesh,
        in_specs=(rows, rows, blocks, blocks, P(), P()),
        out_specs=(blocks, rows, rows),
        check_vma=False,
    )
```

time: 154 us -> 45 us (0.29)
  waiting for transfers between devices: 98.1 us -> 0 us
  Pallas kernels: 0 us -> 43 us
  starting transfers between devices: 36.4 us -> 0 us
  matrix products: 10.2 us -> 0 us
  other arithmetic: 7.28 us -> 0 us
    ppermute x6 -> x0, waiting for transfers between devices: 98.1 us -> none  [passed_along(): return lax.ppermute(block, axis, route)]
    pallas_call x0 -> x2, Pallas kernels: none -> 43 us  [the longest x1 41 us: body(): pl.pallas_call(exchange_kernel, out_shape=handed_on, in_specs=[hbm] * 4 +...]
    ppermute x6 -> x0, starting transfers between devices: 36.4 us -> none  [passed_along(): return lax.ppermute(block, axis, route)]
    dot_general x6 -> x0, matrix products: 10.2 us -> none  [the longest x2 4.01 us: pair_terms(): jnp.dot(image_unit, text_unit.T, preferred_element_type=jnp.float32)]
    convert_element_type x3 -> x0, other arithmetic: 4.7 us -> none  [the longest x2 3.17 us: back_norm(): (inverse * unit_grad - inverse * inverse * inverse * widened * inner_sum)...]
    reduce_sum x2 -> x0, other arithmetic: 1.98 us -> none  [unit_rows(): jnp.sum(widened * widened, axis=1, keepdims=True) + 1e-06]
  transfers between devices with their start and end apart: 6 -> 0, of which waited for: 5 -> 0; matrix products, arithmetic and copies ran while one was open for 5% -> 0% of each run, Pallas kernels for 0% -> 0%
where the time goes in v2:
time: 45 us; the launch traced here: 44.9 us
  Pallas kernels  43 us (96%)
  between operations  1.93 us (4%)
    pallas_call x1, Pallas kernels, body(): pl.pallas_call(exchange_kernel, out_shape=handed_on, in_specs=[hbm] * 4 +...  41 us
    pallas_call x1, Pallas kernels, body(): pl.pallas_call(finish_kernel, out_shape=(pltpu.HBM((ROWS,), f32), pltpu.H...  1.92 us

profile of v2, /device:TPU:1, one launch (start us, length us, event | category | flops | bytes accessed | tf_op | source)
XLA Modules:
  0.0 44.9 jit_solution(5842028169909755325)
XLA Ops:
  1.9 41.0 %exchange_and_grads.1 = (f32[512]{0:T(512)S(1)}, bf16[512,1152]{1,0:T(8,128)(2,1)S(1)}, bf16[512,1152]{1,0:T(8,128)(2,1)S(1)}, bf16[512,1152]{1,0:T(8,128)(2,1)S...) custom-call(bf16[512,1152]{1,0:T(8,128)(2,1)} %img.1, ...), custom_call_target="tpu_custom_call" | custom-call | tf_op jit(solution)/shard_map/exchange_and_grads/pallas_call | solution.py:292
  43.0 1.9 %finish_text_side.1 = (f32[512]{0:T(512)}, bf16[512,1152]{1,0:T(8,128)(2,1)}, bf16[512,1152]{1,0:T(8,128)(2,1)}) custom-call(f32[512]{0:T(512)S(1)} %get-tuple-element.13.loss, bf16[512,1152]{1,0:T(8,128)(2,1)S(1)} %get-tuple-element.14.image_grad, bf16[512,1152]{1,0:T(8,128)(2,1)S(1)} %get-tuple-element.15.own, ...), custom_call_target="tpu_custom_call" | custom-call | tf_op jit(solution)/shard_map/finish_text_side/pallas_call | solution.py:317

commit v3 on v2

--- a/solution.py
+++ b/solution.py
@@ -84,7 +84,7 @@
     id_col = (image_id_col, text_id_col)
     pieces = (
         [(k * C, C) for k in range(FULL + 1)],
-        [(k * C, C) for k in range(FULL)] + [(FULL * C, HALF), (FULL * C + HALF, HALF)],
+        [(k * C, C) for k in range(FULL)] + [(FULL * C, HALF)],
     )
 
     def id_copy(side):
@@ -94,24 +94,25 @@
             device_id=targets[side], device_id_type=MESH,
         )
 
-    def piece_copy(side, k, start, size):
+    def piece_copy(side, k, start, size, source=None):
         rows = pl.ds(start, size)
         return pltpu.make_async_remote_copy(
-            src_ref=sources[side].at[rows], dst_ref=got.at[side, rows],
+            src_ref=(sources[side] if source is None else source).at[rows], dst_ref=got.at[side, rows],
             send_sem=send_sem.at[side, k], recv_sem=recv_sem.at[side, k],
             device_id=targets[side], device_id_type=MESH,
         )
 
     def sends(side):
-        return [id_copy(side)] + [piece_copy(side, k, *piece) for k, piece in enumerate(pieces[side])]
+        rows = [piece_copy(side, k, *piece) for k, piece in enumerate(pieces[side])]
+        return rows[:1] + [id_copy(side)] + rows[1:]
+
+    def last_send():
+        return piece_copy(IMAGE, FULL + 1, FULL * C + HALF, HALF, image_unit)
 
     loads = []
     for side, ref, ids in ((TEXT, img, img_ids), (IMAGE, txt, txt_ids)):
         loads.append(pltpu.make_async_copy(ids, own_ids.at[side], own_id_sem.at[side]))
         loads.append(pltpu.make_async_copy(ref, own[side], own_sem.at[side]))
-    for copy in loads:
-        copy.start()
-
     def start_sends(side):
         for copy in sends(side):
             copy.start()
@@ -122,6 +123,7 @@
     def _():
         pl.semaphore_wait(barrier, n_direct)
 
+    pl.when(image_direct == 1)(lambda: start_sends(IMAGE))
     for i, (acks, partner) in enumerate(((near_acks, near_to), (far_acks, far_to))):
 
         @pl.when(acks == 1)
@@ -129,14 +131,20 @@
             pl.semaphore_signal(ack_sem.at[i], inc=1, device_id=partner, device_id_type=MESH)
 
     image_ack = jnp.where(core == 0, 1, 0)
-    pl.when(image_direct == 1)(lambda: start_sends(IMAGE))
     pl.when(text_direct == 1)(lambda: start_sends(TEXT))
-    for side, direct, ack in ((IMAGE, image_direct, image_ack), (TEXT, text_direct, 1 - image_ack)):
-
-        @pl.when(direct == 0)
-        def _():
-            pl.semaphore_wait(ack_sem.at[ack], 1)
-            start_sends(side)
+    for copy in loads:
+        copy.start()
+    def send_when_acknowledged(side, ack):
+        pl.semaphore_wait(ack_sem.at[ack], 1)
+        start_sends(side)
+
+    @pl.when(image_direct == 0)
+    def _():
+        send_when_acknowledged(IMAGE, image_ack)
+
+    @pl.when((1 - text_direct) * (1 - last) == 1)
+    def _():
+        send_when_acknowledged(TEXT, 1 - image_ack)
 
     scale = jnp.exp(jnp.full((1, C), log_scale[0], jnp.float32))
     bias = jnp.full((1, C), logit_bias[0], jnp.float32)
@@ -160,6 +168,13 @@
             r = inverse_norm(x)
             inv[side][piece, :] = jnp.broadcast_to(r, (C, C))
             unit[side][piece, :] = (x * r).astype(jnp.bfloat16)
+
+        if side == TEXT:
+            last_send().start()
+
+            @pl.when((1 - text_direct) * last == 1)
+            def _():
+                send_when_acknowledged(TEXT, 1 - image_ack)
 
     loss_acc[...] = jnp.zeros_like(loss_acc)
     for side in (TEXT, IMAGE):
@@ -223,10 +238,10 @@
 
     pl.when(first == 0)(finish_text)
 
-    for side in (TEXT, IMAGE):
-        for copy in sends(side):
-            copy.wait_send()
-    last_unit[...] = arrived(IMAGE, FULL + 1, FULL * C + HALF, HALF)
+    for copy in sends(TEXT) + sends(IMAGE) + [last_send()]:
+        copy.wait_send()
+    last_send().wait_recv()
+    last_unit[...] = got[IMAGE, pl.ds(FULL * C + HALF, HALF), :]
 
 
 def finish_kernel(

time: 45 us -> 44.9 us (level)
  no operation moved by 1% of the time
where the time goes in v3:
time: 44.9 us; the launch traced here: 44.7 us
  Pallas kernels  42.8 us (95%)
  between operations  1.93 us (4%)
    pallas_call x1, Pallas kernels, body(): pl.pallas_call(exchange_kernel, out_shape=handed_on, in_specs=[hbm] * 4 +...  40.9 us
    pallas_call x1, Pallas kernels, body(): pl.pallas_call(finish_kernel, out_shape=(pltpu.HBM((ROWS,), f32), pltpu.H...  1.92 us

profile of v3, /device:TPU:1, one launch (start us, length us, event | category | flops | bytes accessed | tf_op | source)
XLA Modules:
  0.0 44.7 jit_solution(1138373486496442265)
XLA Ops:
  1.9 40.9 %exchange_and_grads.1 = (f32[512]{0:T(512)S(1)}, bf16[512,1152]{1,0:T(8,128)(2,1)S(1)}, bf16[512,1152]{1,0:T(8,128)(2,1)S(1)}, bf16[512,1152]{1,0:T(8,128)(2,1)S...) custom-call(bf16[512,1152]{1,0:T(8,128)(2,1)} %img.1, ...), custom_call_target="tpu_custom_call" | custom-call | tf_op jit(solution)/shard_map/exchange_and_grads/pallas_call | solution.py:307
  42.8 1.9 %finish_text_side.1 = (f32[512]{0:T(512)}, bf16[512,1152]{1,0:T(8,128)(2,1)}, bf16[512,1152]{1,0:T(8,128)(2,1)}) custom-call(f32[512]{0:T(512)S(1)} %get-tuple-element.13.loss, bf16[512,1152]{1,0:T(8,128)(2,1)S(1)} %get-tuple-element.14.image_grad, bf16[512,1152]{1,0:T(8,128)(2,1)S(1)} %get-tuple-element.15.own, ...), custom_call_target="tpu_custom_call" | custom-call | tf_op jit(solution)/shard_map/finish_text_side/pallas_call | solution.py:332

commit v4 on v2

--- a/solution.py
+++ b/solution.py
@@ -44,7 +44,7 @@
 
 def exchange_kernel(
     img, txt, img_ids, txt_ids, log_scale, logit_bias,
-    loss, image_grad, text_own, text_unit, text_inv, text_base, last_unit, text_id_col, last_id_row, constants,
+    loss, image_grad, text_own, text_unit, text_inv, text_coef, text_base, last_unit, text_id_col, last_id_row, constants,
     image_own, image_unit, image_inv, image_acc, got, own_ids, got_ids, image_id_col, id_row, loss_acc,
     own_sem, own_id_sem, send_sem, recv_sem, id_send_sem, id_recv_sem, ack_sem,
 ):
@@ -159,7 +159,13 @@
             x = own[side][piece, :].astype(jnp.float32)
             r = inverse_norm(x)
             inv[side][piece, :] = jnp.broadcast_to(r, (C, C))
-            unit[side][piece, :] = (x * r).astype(jnp.bfloat16)
+            rounded = (x * r).astype(jnp.bfloat16)
+            unit[side][piece, :] = rounded
+            if side == IMAGE:
+                u = rounded.astype(jnp.float32)
+                squares = jnp.maximum(jnp.sum(u * u, axis=1, keepdims=True), 1e-30)
+                ratio = jnp.sum(x * u, axis=1, keepdims=True) / squares
+                text_coef[piece, :] = jnp.broadcast_to(r * r * r * ratio, (C, C))
 
     loss_acc[...] = jnp.zeros_like(loss_acc)
     for side in (TEXT, IMAGE):
@@ -230,7 +236,7 @@
 
 
 def finish_kernel(
-    loss, image_grad, own, unit, inv, base, last_unit, id_col, last_id_row, constants,
+    loss, image_grad, own, unit, inv, coef, base, last_unit, id_col, last_id_row, constants,
     loss_out, image_out, text_out,
     stage, sem,
 ):
@@ -258,7 +264,7 @@
         rows = pl.ds(b * BLOCK, BLOCK)
         r = inv[rows, 0:1]
         h = jnp.dot(slopes, other, preferred_element_type=jnp.float32)
-        grad = base[rows, :] + r * h - (r * r * inner) * own[rows, :].astype(jnp.float32)
+        grad = base[rows, :] + r * h - (coef[rows, 0:1] * inner) * own[rows, :].astype(jnp.float32)
         stage[rows, :] = grad.astype(jnp.bfloat16)
         copy = pltpu.make_async_copy(stage.at[rows], text_out.at[rows], sem.at[2 + b])
         copy.start()
@@ -282,6 +288,7 @@
         pltpu.VMEM((ROWS, D), bf16),
         pltpu.VMEM((ROWS, D), bf16),
         pltpu.VMEM((ROWS, D), bf16),
+        pltpu.VMEM((ROWS, C), f32),
         pltpu.VMEM((ROWS, C), f32),
         pltpu.VMEM((ROWS, D), f32),
         pltpu.VMEM((HALF, D), bf16),

time: 45 us -> 45 us (level)
  no operation moved by 1% of the time
where the time goes in v4:
time: 45 us; the launch traced here: 44.9 us
  Pallas kernels  43 us (96%)
  between operations  1.93 us (4%)
    pallas_call x1, Pallas kernels, body(): pl.pallas_call(exchange_kernel, out_shape=handed_on, in_specs=[hbm] * 4 +...  41 us
    pallas_call x1, Pallas kernels, body(): pl.pallas_call(finish_kernel, out_shape=(pltpu.HBM((ROWS,), f32), pltpu.H...  1.92 us

profile of v4, /device:TPU:1, one launch (start us, length us, event | category | flops | bytes accessed | tf_op | source)
XLA Modules:
  0.0 44.9 jit_solution(13785134474898266993)
XLA Ops:
  1.9 41.0 %exchange_and_grads.1 = (f32[512]{0:T(512)S(1)}, bf16[512,1152]{1,0:T(8,128)(2,1)S(1)}, bf16[512,1152]{1,0:T(8,128)(2,1)S(1)}, bf16[512,1152]{1,0:T(8,128)(2,1)S...) custom-call(bf16[512,1152]{1,0:T(8,128)(2,1)} %img.1, ...), custom_call_target="tpu_custom_call" | custom-call | tf_op jit(solution)/shard_map/exchange_and_grads/pallas_call | solution.py:299
  43.0 1.9 %finish_text_side.1 = (f32[512]{0:T(512)}, bf16[512,1152]{1,0:T(8,128)(2,1)}, bf16[512,1152]{1,0:T(8,128)(2,1)}) custom-call(f32[512]{0:T(512)S(1)} %get-tuple-element.14.loss, bf16[512,1152]{1,0:T(8,128)(2,1)S(1)} %get-tuple-element.15.image_grad, bf16[512,1152]{1,0:T(8,128)(2,1)S(1)} %get-tuple-element.16.own, ...), custom_call_target="tpu_custom_call" | custom-call | tf_op jit(solution)/shard_map/finish_text_side/pallas_call | solution.py:324
